TPU v7x, 512 devices: a whole 4x4x16 slice. The times are simulated.
512 devices in a mesh: dp: 64 (over x_lo, z, core), fsdp: 8 (over y, x_hi).
Axes of the slice: x: 4 (x_hi: 2, x_lo: 2; x = x_hi * 2 + x_lo), y: 4, z: 16, core: 2. Of those that a mesh axis runs over, the one named last changes fastest.
Arguments:
- tokens: bfloat16 [65536, 1024], P('dp'), may hold values from -8 to 8
- teacher: bfloat16 [512, 6144], P('dp'), may hold values from -8 to 8
- norm_gain: float32 [1024], replicated, may hold values from 0.25 to 1.75
- w_in: bfloat16 [1024, 4096], P(None, 'fsdp'), may hold values from -0.1875 to 0.1875
- b_in: float32 [4096], P('fsdp'), may hold values from -3 to 3
- w_out: bfloat16 [1024, 4096], P(None, 'fsdp'), may hold values from -0.09375 to 0.09375
- b_out: float32 [1024], replicated, may hold values from -3 to 3
- final_gain: float32 [1024], replicated, may hold values from 0.25 to 1.75
Outputs:
- loss_value: float32 [], replicated
- grad_in: bfloat16 [1024, 4096], P('dp', 'fsdp')
- grad_out: bfloat16 [1024, 4096], P('dp', 'fsdp')
All inputs are finite; a program needn't handle non-finite values.
Results may differ from a plain program's by a relative error of at most 0.008.
Values may be sent and summed in bfloat16 or wider, within the bound.
A program may use at most 64 MiB of HBM per device.

v0:
```python
import jax
import jax.numpy as jnp
from jax import lax
from jax.sharding import PartitionSpec as P

loss_scale = 4096.0


def gelu_tanh(values):
    inner = 0.7978845608 * (values + 0.044715 * values * values * values)
    return 0.5 * values * (1.0 + jnp.tanh(inner))


def gelu_slope(values):
    inner = 0.7978845608 * (values + 0.044715 * values * values * values)
    tangent = jnp.tanh(inner)
    return 0.5 * (1.0 + tangent) + 0.5 * values * (1.0 - tangent * tangent) * 0.7978845608 * (
        1.0 + 3.0 * 0.044715 * values * values
    )


def layer_norm(values, gain_vec):
    centered = values - jnp.mean(values, axis=-1, keepdims=True)
    inv_std = lax.rsqrt(jnp.mean(centered * centered, axis=-1, keepdims=True) + 1e-05)
    normed = centered * inv_std
    return (normed * gain_vec, normed, inv_std)


def contract_last(left_side, right_side):
    return lax.dot_general(
        left_side, right_side, (((1,), (1,)), ((), ())), preferred_element_type=jnp.float32
    )


def contract_first(left_side, right_side):
    return lax.dot_general(
        left_side, right_side, (((0,), (0,)), ((), ())), preferred_element_type=jnp.float32
    )


def body(tokens, teacher, norm_gain, w_in, b_in, w_out, b_out, final_gain):
    dp_size = lax.axis_size("dp")
    fsdp_size = lax.axis_size("fsdp")
    block_rows = teacher.shape[0]
    model_width = tokens.shape[1]
    per_image = tokens.shape[0] // block_rows
    image_count = block_rows * dp_size
    token_values = tokens.astype(jnp.float32)
    normed_tokens = layer_norm(token_values, norm_gain)[0].astype(jnp.bfloat16)
    pre_act = jnp.dot(normed_tokens, w_in, preferred_element_type=jnp.float32) + b_in
    hidden = pre_act.shape[1]
    pooled = (
        gelu_tanh(pre_act).reshape(block_rows, per_image, hidden).mean(axis=1).astype(jnp.bfloat16)
    )
    token_mean = token_values.reshape(block_rows, per_image, model_width).mean(axis=1)
    partial_value = contract_last(pooled, w_out)
    embedding = token_mean + lax.psum(partial_value, "fsdp") + b_out
    scaled_unit, normed_embed, inv_std = layer_norm(embedding, final_gain)
    unit_norm = jnp.sqrt(jnp.sum(scaled_unit * scaled_unit, axis=-1, keepdims=True) + 1e-06)
    unit_dir = scaled_unit / unit_norm
    student = unit_dir.astype(jnp.bfloat16)
    teacher_f = teacher.astype(jnp.float32)
    target = (
        teacher_f / jnp.sqrt(jnp.sum(teacher_f * teacher_f, axis=-1, keepdims=True) + 1e-06)
    ).astype(jnp.bfloat16)
    rows_each = block_rows // fsdp_size
    first_row = lax.axis_index("fsdp") * rows_each
    own_student = lax.dynamic_slice_in_dim(student, first_row, rows_each, 0)
    own_target = lax.dynamic_slice_in_dim(target, first_row, rows_each, 0)
    piece_student = lax.all_gather(student, "dp", axis=0, tiled=True)
    piece_target = lax.all_gather(target, "dp", axis=0, tiled=True)
    resid = contract_last(own_student, piece_student) - contract_last(own_target, piece_target)
    grad_acc = jnp.dot(
        resid.astype(jnp.bfloat16), piece_student, preferred_element_type=jnp.float32
    )
    sum_part = jnp.sum(resid * resid)
    grad_sum = lax.all_gather(grad_acc, "fsdp", axis=0, tiled=True)
    loss_value = lax.psum(sum_part, ("dp", "fsdp")) / image_count
    dstudent = loss_scale * 4.0 / image_count * grad_sum
    dunit = (dstudent - unit_dir * jnp.sum(unit_dir * dstudent, axis=-1, keepdims=True)) / unit_norm
    gain_grad = dunit * final_gain
    dembed = inv_std * (
        gain_grad
        - jnp.mean(gain_grad, axis=-1, keepdims=True)
        - normed_embed * jnp.mean(gain_grad * normed_embed, axis=-1, keepdims=True)
    )
    dembed_b = dembed.astype(jnp.bfloat16)
    dpooled = jnp.dot(dembed_b, w_out, preferred_element_type=jnp.float32)
    slope = gelu_slope(pre_act.reshape(block_rows, per_image, hidden))
    dhidden = (
        (dpooled[:, None, :] / per_image * slope)
        .reshape(block_rows * per_image, hidden)
        .astype(jnp.bfloat16)
    )
    in_term = contract_first(normed_tokens, dhidden)
    out_term = contract_first(dembed_b, pooled)
    shares = lax.psum_scatter(
        jnp.concatenate([in_term, out_term], axis=1), "dp", scatter_dimension=0, tiled=True
    )
    grad_in = shares[:, :hidden].astype(jnp.bfloat16)
    grad_out = shares[:, hidden:].astype(jnp.bfloat16)
    return (loss_value, grad_in, grad_out)


def solution(mesh):
    return jax.shard_map(
        body,
        mesh=mesh,
        in_specs=(
            P("dp", None),
            P("dp", None),
            P(),
            P(None, "fsdp"),
            P("fsdp"),
            P(None, "fsdp"),
            P(),
            P(),
        ),
        out_specs=(P(), P("dp", "fsdp"), P("dp", "fsdp")),
        check_vma=False,
    )
```

profile of v0, /device:TPU:4, one launch (start us, length us, event | category | flops | bytes accessed | tf_op | source)
XLA Modules:
  0.0 595.0 jit_solution(14809419079678232370)
XLA Ops:
  7.2 0.0 copy-start
  7.2 0.0 copy-start.1
  7.2 0.0 all-gather.4.cloned.1.call-start
  7.2 2.1 convert_reduce_fusion
  9.3 0.2 copy-done.1
  9.5 0.0 copy-start.8
  9.5 0.0 copy-start.9
  9.5 0.4 bitcast_reduce_fusion
  9.9 0.7 multiply_reduce_fusion
  10.6 0.0 copy-done
  10.6 0.0 copy-done.8
  10.6 0.0 copy-done.9
  10.6 0.0 copy-start.4
  10.6 0.0 copy-start.7
  10.7 0.0 copy-start.6
  10.7 0.0 copy-start.5
  10.7 3.3 bitcast_reduce_fusion.1
  13.9 0.0 copy-done.4
  13.9 0.4 fusion.16
  14.3 40.4 %psum.14 = f32[8,1024]{1,0:T(8,128)S(1)} all-reduce(f32[8,1024]{1,0:T(8,128)S(1)} %fusion.16), channel_id=1, replica_groups=mesh['dp'=64,'fsdp'=8] {'fsdp'}, use_global_device_ids=true, to_apply=%region_4.0 | all-reduce | flops 8192 | bytes 65536 | tf_op jit(solution)/shard_map/psum | solution.py:57
  54.7 0.0 copy-done.7
  54.7 0.1 fusion.25
  54.9 0.2 multiply_reduce_fusion.4
  55.1 0.0 copy-done.6
  55.1 0.2 multiply_reduce_fusion.3
  55.3 0.7 fusion.21
  56.0 0.0 all-gather.4.cloned.1.call-update
  56.0 0.0 all-gather.6.cloned.1.call-start
  56.1 0.0 copy-done.5
  56.1 0.2 fusion.7
  56.2 0.7 fusion.8
  57.0 0.0 all-gather.6.cloned.1.call-update
  57.0 0.0 reduce-scatter.4.cloned.1.call-start
  57.0 120.5 %all-gather.4.cloned.1.call-done = bf16[512,1024]{1,0:T(8,128)(2,1)} async-done(((bf16[8,1024]{1,0:T(8,128)(2,1)}), bf16[512,1024]{1,0:T(8,128)(2,1)}) %all-gather.4.cloned.1.call-update) | async-done | bytes 1048592 | tf_op jit(solution)/shard_map/all_gather | solution.py:70
  177.5 1.6 fusion.12
  179.1 124.2 %all-gather.6.cloned.1.call-done = bf16[512,6144]{1,0:T(8,128)(2,1)} async-done(((bf16[8,6144]{1,0:T(8,128)(2,1)}), bf16[512,6144]{1,0:T(8,128)(2,1)}) %all-gather.6.cloned.1.call-update) | async-done | bytes 6291472 | tf_op jit(solution)/shard_map/all_gather | solution.py:71
  303.3 0.0 copy-start.2
  303.3 4.6 fusion.9
  308.0 0.6 subtract_convert_fusion
  308.6 0.0 copy-done.2
  308.6 0.2 fusion.27
  308.9 34.2 %all-gather = f32[8192]{0:T(1024)S(1)} all-gather(f32[1024]{0:T(1024)S(1)} %bitcast.24), channel_id=2, replica_groups=mesh['dp'=64,'fsdp'=8] {'fsdp'}, dimensions={0}, use_global_device_ids=true | all-gather | bytes 36864 | tf_op jit(solution)/shard_map/all_gather | solution.py:77
  343.1 0.0 copy-start.3
  343.1 0.2 multiply_reduce_fusion.2
  343.3 0.2 fusion.24
  343.5 1.7 convolution_multiply_fusion
  345.2 0.5 fusion.15
  345.7 0.0 copy-done.3
  345.7 1.4 fusion.6
  347.1 1.5 fusion.22
  348.6 2.5 pad_maximum_fusion
  351.1 5.3 copy.15
  356.5 0.0 reduce-scatter.4.cloned.1.call-update
  356.5 99.2 %psum.15 = f32[]{:T(128)} all-reduce(f32[]{:T(128)} %get-tuple-element.17), channel_id=1, replica_groups=mesh['dp'=64,'fsdp'=8] {'dp','fsdp'}, use_global_device_ids=true, to_apply=%region_10.0 | all-reduce | flops 1 | bytes 8 | tf_op jit(solution)/shard_map/psum | solution.py:78
  456.4 128.5 %reduce-scatter.4.cloned.1.call-done = f32[16,1024]{1,0:T(8,128)} async-done(((f32[1024,1024]{1,0:T(8,128)}), f32[16,1024]{1,0:T(8,128)}) %reduce-scatter.4.cloned.1.call-update) | async-done | bytes 65552
  584.9 1.0 copy.16
  586.0 0.7 copy.14
  586.7 0.7 copy.13
  (11 shorter events, 0.1 us)
Async XLA Ops:
  7.2 3.4 copy-start
  7.2 2.3 copy-start.1
  7.2 170.3 %all-gather.4.cloned.1.call-start = ((), (), s32[]{:S(2)}) async-start(), calls=%async_computation.1 | async-start | bytes 1064960 | tf_op jit(solution)/shard_map/all_gather | solution.py:70
  9.5 1.1 copy-start.8
  9.5 1.1 copy-start.9
  10.6 3.3 copy-start.4
  10.6 44.1 %copy-start.7 = (f32[1024]{0:T(1024)S(1)}, f32[1024]{0:T(1024)}, u32[]{:S(2)}) copy-start(f32[1024]{0:T(1024)} %param.14) | copy-start | bytes 12292
  10.7 44.4 %copy-start.6 = (f32[1024]{0:T(1024)S(1)}, f32[1024]{0:T(1024)}, u32[]{:S(2)}) copy-start(f32[1024]{0:T(1024)} %param.15) | copy-start | bytes 12292
  10.7 45.4 %copy-start.5 = (bf16[8,6144]{1,0:T(8,128)(2,1)S(1)}, bf16[8,6144]{1,0:T(8,128)(2,1)}, u32[]{:S(2)}) copy-start(bf16[8,6144]{1,0:T(8,128)(2,1)} %param.9) | copy-start | bytes 294916
  56.0 247.3 %all-gather.6.cloned.1.call-start = ((), (), s32[]{:S(2)}) async-start(), calls=%async_computation.2 | async-start | bytes 6389760 | tf_op jit(solution)/shard_map/all_gather | solution.py:71
  57.0 527.9 %reduce-scatter.4.cloned.1.call-start = ((), (), s32[]{:S(2)}) async-start(), calls=%async_computation.3 | async-start | bytes 4259840
  303.3 5.3 copy-start.2
  343.1 2.6 copy-start.3
Sparse Core Ops, SparseCore 0:
  56.1 121.3 all-gather.3
  179.7 123.6 all-gather.5
  356.6 228.2 reduce-scatter.3
where the time goes:
time: 595 us
  waiting for transfers between devices  373 us (63%)
  blocking collectives  174 us (29%)
  between operations  15.7 us (3%)
  matrix products  13.8 us (2%)
  other arithmetic  10.2 us (2%)
  local copies, waits for them, and re-layouts  8 us (1%)
    unnamed x4, waiting for transfers between devices  129 us
    all_gather x1, waiting for transfers between devices, body(): piece_target = lax.all_gather(target, 'dp', axis=0, tiled=True)  124 us
    all_gather x1, waiting for transfers between devices, body(): piece_student = lax.all_gather(student, 'dp', axis=0, tiled=True)  120 us
    psum x1, blocking collectives, body(): loss_value = lax.psum(sum_part, ('dp', 'fsdp')) / image_count  99.2 us
    psum x1, blocking collectives, body(): embedding = token_mean + lax.psum(partial_value, 'fsdp') + b_out  40.4 us
    all_gather x1, blocking collectives, body(): grad_sum = lax.all_gather(grad_acc, 'fsdp', axis=0, tiled=True)  34.2 us
  transfers between devices with their start and end apart: 3, of which 3 were waited for; matrix products, arithmetic and copies ran while one was open for 0% of the time, Pallas kernels for 0%

commit v1 on v0

--- a/solution.py
+++ b/solution.py
@@ -54,7 +54,7 @@
     )
     token_mean = token_values.reshape(block_rows, per_image, model_width).mean(axis=1)
     partial_value = contract_last(pooled, w_out)
-    embedding = token_mean + lax.psum(partial_value, "fsdp") + b_out
+    embedding = token_mean + jnp.sum(lax.all_gather(partial_value, "fsdp"), axis=0) + b_out
     scaled_unit, normed_embed, inv_std = layer_norm(embedding, final_gain)
     unit_norm = jnp.sqrt(jnp.sum(scaled_unit * scaled_unit, axis=-1, keepdims=True) + 1e-06)
     unit_dir = scaled_unit / unit_norm

time: 595 us -> 593 us (level)
    psum x1 -> x0, blocking collectives: 40.4 us -> none  [body(): embedding = token_mean + lax.psum(partial_value, 'fsdp') + b_out]
    all_gather x0 -> x1, blocking collectives: none -> 35.3 us  [body(): lax.all_gather(partial_value, 'fsdp')]
where the time goes in v1:
time: 593 us
  waiting for transfers between devices  376 us (63%)
  blocking collectives  169 us (28%)
  between operations  15.7 us (3%)
  matrix products  13.8 us (2%)
  other arithmetic  10.2 us (2%)
  local copies, waits for them, and re-layouts  8 us (1%)
    unnamed x4, waiting for transfers between devices  129 us
    all_gather x1, waiting for transfers between devices, body(): piece_target = lax.all_gather(target, 'dp', axis=0, tiled=True)  124 us
    all_gather x1, waiting for transfers between devices, body(): piece_student = lax.all_gather(student, 'dp', axis=0, tiled=True)  123 us
    psum x1, blocking collectives, body(): loss_value = lax.psum(sum_part, ('dp', 'fsdp')) / image_count  99.3 us
    all_gather x1, blocking collectives, body(): lax.all_gather(partial_value, 'fsdp')  35.3 us
    all_gather x1, blocking collectives, body(): grad_sum = lax.all_gather(grad_acc, 'fsdp', axis=0, tiled=True)  34.2 us
  transfers between devices with their start and end apart: 3, of which 3 were waited for; matrix products, arithmetic and copies ran while one was open for 0% of the time, Pallas kernels for 0%

profile of v1, /device:TPU:4, one launch (start us, length us, event | category | flops | bytes accessed | tf_op | source)
XLA Modules:
  0.0 592.7 jit_solution(9736178518718344872)
XLA Ops:
  7.2 0.0 copy-start
  7.2 0.0 copy-start.1
  7.2 0.0 all-gather.5.cloned.1.call-start
  7.2 2.1 convert_reduce_fusion
  9.3 0.2 copy-done.1
  9.5 0.0 copy-start.8
  9.5 0.0 copy-start.9
  9.5 0.4 bitcast_reduce_fusion
  9.9 0.7 multiply_reduce_fusion
  10.6 0.0 copy-done
  10.6 0.0 copy-done.8
  10.6 0.0 copy-done.9
  10.6 0.0 copy-start.4
  10.6 0.0 copy-start.7
  10.7 0.0 copy-start.6
  10.7 0.0 copy-start.5
  10.7 3.3 bitcast_reduce_fusion.1
  13.9 0.0 copy-done.4
  13.9 0.4 fusion.16
  14.3 35.3 %all-gather = f32[64,1024]{1,0:T(8,128)S(1)} all-gather(f32[8,1024]{1,0:T(8,128)S(1)} %fusion.16), channel_id=2, replica_groups=mesh['dp'=64,'fsdp'=8] {'fsdp'}, dimensions={0}, use_global_device_ids=true | all-gather | bytes 294912 | tf_op jit(solution)/shard_map/all_gather | solution.py:57
  49.6 0.0 copy-done.7
  49.6 0.1 fusion.25
  49.7 0.2 multiply_reduce_fusion.4
  49.9 0.0 copy-done.6
  49.9 0.2 multiply_reduce_fusion.3
  50.2 0.7 fusion.21
  50.8 0.0 all-gather.5.cloned.1.call-update
  50.9 0.0 all-gather.7.cloned.1.call-start
  50.9 0.0 copy-done.5
  50.9 0.2 fusion.7
  51.1 0.7 fusion.8
  51.8 0.0 all-gather.7.cloned.1.call-update
  51.9 0.0 reduce-scatter.4.cloned.1.call-start
  51.9 123.3 %all-gather.5.cloned.1.call-done = bf16[512,1024]{1,0:T(8,128)(2,1)} async-done(((bf16[8,1024]{1,0:T(8,128)(2,1)}), bf16[512,1024]{1,0:T(8,128)(2,1)}) %all-gather.5.cloned.1.call-update) | async-done | bytes 1048592 | tf_op jit(solution)/shard_map/all_gather | solution.py:70
  175.2 1.6 fusion.12
  176.9 124.2 %all-gather.7.cloned.1.call-done = bf16[512,6144]{1,0:T(8,128)(2,1)} async-done(((bf16[8,6144]{1,0:T(8,128)(2,1)}), bf16[512,6144]{1,0:T(8,128)(2,1)}) %all-gather.7.cloned.1.call-update) | async-done | bytes 6291472 | tf_op jit(solution)/shard_map/all_gather | solution.py:71
  301.1 0.0 copy-start.2
  301.1 4.6 fusion.9
  305.7 0.6 subtract_convert_fusion
  306.3 0.0 copy-done.2
  306.3 0.2 fusion.27
  306.6 34.2 %all-gather.1 = f32[8192]{0:T(1024)S(1)} all-gather(f32[1024]{0:T(1024)S(1)} %bitcast.26), channel_id=3, replica_groups=mesh['dp'=64,'fsdp'=8] {'fsdp'}, dimensions={0}, use_global_device_ids=true | all-gather | bytes 36864 | tf_op jit(solution)/shard_map/all_gather | solution.py:77
  340.8 0.0 copy-start.3
  340.8 0.2 multiply_reduce_fusion.2
  341.0 0.2 fusion.24
  341.2 1.7 convolution_multiply_fusion
  343.0 0.5 fusion.15
  343.5 0.0 copy-done.3
  343.5 1.4 fusion.6
  344.9 1.5 fusion.22
  346.3 2.5 pad_maximum_fusion
  348.8 5.3 copy.17
  354.2 0.0 reduce-scatter.4.cloned.1.call-update
  354.2 99.3 %psum.7 = f32[]{:T(128)} all-reduce(f32[]{:T(128)} %get-tuple-element.20), channel_id=1, replica_groups=mesh['dp'=64,'fsdp'=8] {'dp','fsdp'}, use_global_device_ids=true, to_apply=%region_10.0 | all-reduce | flops 1 | bytes 8 | tf_op jit(solution)/shard_map/psum | solution.py:78
  454.2 128.5 %reduce-scatter.4.cloned.1.call-done = f32[16,1024]{1,0:T(8,128)} async-done(((f32[1024,1024]{1,0:T(8,128)}), f32[16,1024]{1,0:T(8,128)}) %reduce-scatter.4.cloned.1.call-update) | async-done | bytes 65552
  582.7 1.0 copy.18
  583.7 0.7 copy.16
  584.4 0.7 copy.15
  (12 shorter events, 0.1 us)
Async XLA Ops:
  7.2 3.4 copy-start
  7.2 2.3 copy-start.1
  7.2 168.1 %all-gather.5.cloned.1.call-start = ((), (), s32[]{:S(2)}) async-start(), calls=%async_computation.1 | async-start | bytes 1064960 | tf_op jit(solution)/shard_map/all_gather | solution.py:70
  9.5 1.1 copy-start.8
  9.5 1.1 copy-start.9
  10.6 3.3 copy-start.4
  10.6 39.0 %copy-start.7 = (f32[1024]{0:T(1024)S(1)}, f32[1024]{0:T(1024)}, u32[]{:S(2)}) copy-start(f32[1024]{0:T(1024)} %param.14) | copy-start | bytes 12292
  10.7 39.3 %copy-start.6 = (f32[1024]{0:T(1024)S(1)}, f32[1024]{0:T(1024)}, u32[]{:S(2)}) copy-start(f32[1024]{0:T(1024)} %param.15) | copy-start | bytes 12292
  10.7 40.3 %copy-start.5 = (bf16[8,6144]{1,0:T(8,128)(2,1)S(1)}, bf16[8,6144]{1,0:T(8,128)(2,1)}, u32[]{:S(2)}) copy-start(bf16[8,6144]{1,0:T(8,128)(2,1)} %param.9) | copy-start | bytes 294916
  50.9 250.2 %all-gather.7.cloned.1.call-start = ((), (), s32[]{:S(2)}) async-start(), calls=%async_computation.2 | async-start | bytes 6389760 | tf_op jit(solution)/shard_map/all_gather | solution.py:71
  51.9 530.8 %reduce-scatter.4.cloned.1.call-start = ((), (), s32[]{:S(2)}) async-start(), calls=%async_computation.3 | async-start | bytes 4259840
  301.1 5.3 copy-start.2
  340.8 2.6 copy-start.3
Sparse Core Ops, SparseCore 0:
  51.0 124.2 all-gather.4
  177.4 123.6 all-gather.6
  354.3 228.2 reduce-scatter.3
